TPU v7x, 128 devices: a whole 4x4x4 slice. The times are simulated.
128 devices in a mesh: comp: 8 (over z, core), lat: 16 (over y, x).
Axes of the slice: x: 4, y: 4, z: 4, core: 2. Of those that a mesh axis runs over, the one named last changes fastest.
Arguments:
- energy: float32 [1800, 64, 1536], P('comp', 'lat'), may hold values from 0.05 to 1
- sea_mask: int32 [64, 1536], replicated, may hold values from 0 to 1, as said below
- depth_class: int32 [64, 1536], replicated, may hold values from 0 to 7
- group_speed: float32 [50, 8], replicated, may hold values from 0.08 to 0.6
- wind_input: float32 [1800], replicated, may hold values from 0.05 to 0.5
- whitecap: float32 [1800], replicated, may hold values from 0.2 to 1
- pair_in: bfloat16 [1800, 1800], replicated, may hold values from -0.125 to 0.125
- pair_out: bfloat16 [1800, 1800], replicated, may hold values from -0.125 to 0.125
Outputs:
- energy_next: float32 [1800, 64, 1536], P('comp', 'lat')
Inputs may be any that keep to these rules, and one draw needn't show every extreme that they name: `sea_mask`: cut every tile of 4 latitude rows into consecutive slices of 48 cells in row-major order; the slices at one slice position in all tiles together hold exactly 336 sea cells.
All inputs are finite; a program needn't handle non-finite values.
Results may differ from a plain program's by a relative error of at most 0.00065.
Values sent between devices are 32-bit elements; how exact they have to be, the bound alone decides.
A program may use at most 192 MiB of HBM per device.

v0:
```python
import math

import jax
import jax.numpy as jnp
from jax import lax
from jax.sharding import PartitionSpec as P

NDIR = 36
SUB = 2


time_step = 0.5


def extended_2(x, sides, width):
    for axis, dim in sides:
        size, length = (lax.axis_size(axis), x.shape[dim])
        up = [(i, (i + 1) % size) for i in range(size - 1)]
        down = [(j, i) for i, j in up]
        last = lax.slice_in_dim(x, length - width, length, axis=dim)
        initial = lax.slice_in_dim(x, 0, width, axis=dim)
        before = lax.ppermute(last, axis, up)
        after = lax.ppermute(initial, axis, down)
        x = jnp.concatenate([before, x, after], axis=dim)
    return x


def upwind(extended, zonal_speed, meridional, sea_cells):
    spectra = extended[:, 1:-1]
    south_cells = extended[:, :-2]
    north_cells = extended[:, 2:]
    zero_column = jnp.zeros_like(spectra[:, :, :1])
    west_cells = jnp.concatenate([zero_column, spectra[:, :, :-1]], axis=2)
    east_cells = jnp.concatenate([spectra[:, :, 1:], zero_column], axis=2)
    advected = (
        spectra
        - jnp.maximum(zonal_speed, 0.0) * (spectra - west_cells)
        - jnp.minimum(zonal_speed, 0.0) * (east_cells - spectra)
    )
    advected = (
        advected
        - jnp.maximum(meridional, 0.0) * (spectra - south_cells)
        - jnp.minimum(meridional, 0.0) * (north_cells - spectra)
    )
    return advected * sea_cells


def per_device(energy, sea_mask, depth_class, group_speed, wind_input, whitecap, pair_in, pair_out):
    comp_count = lax.axis_size("comp")
    lat_count = lax.axis_size("lat")
    comp_local = energy.shape[0]
    tile_rows = energy.shape[1]
    lon_cells = energy.shape[2]
    cell_count = tile_rows * lon_cells
    lat_place = lax.axis_index("lat")
    comp_place = lax.axis_index("comp")
    comp_ids = comp_place * comp_local + jnp.arange(comp_local)
    freq_ids = comp_ids // NDIR
    dir_ids = comp_ids % NDIR
    angles = 2.0 * math.pi * (dir_ids.astype(jnp.float32) + 0.5) / NDIR
    cosine = jnp.cos(angles)
    sine_dir = jnp.sin(angles)
    speed_table = group_speed[freq_ids]
    padded_class = jnp.pad(depth_class, ((SUB, SUB), (0, 0)))
    padded_sea = jnp.pad(sea_mask, ((SUB, SUB), (0, 0))).astype(jnp.float32)

    def band_rows(rows_table, margin):
        return lax.dynamic_slice_in_dim(
            rows_table, lat_place * tile_rows + SUB - margin, tile_rows + 2 * margin, 0
        )

    sea_local = band_rows(padded_sea, 0)
    spectra = energy * sea_local[None]
    classes = band_rows(padded_class, 0)
    speed_cells = jnp.zeros((comp_local,) + classes.shape, jnp.float32)
    for depth_level in range(group_speed.shape[1]):
        speed_cells = speed_cells + jnp.where(
            classes[None] == depth_level, speed_table[:, depth_level][:, None, None], 0.0
        )
    zonal_speed = speed_cells * cosine[:, None, None]
    meridional = speed_cells * sine_dir[:, None, None]
    for substep in range(SUB):
        extended = extended_2(spectra, (("lat", 1),), 1)
        spectra = upwind(extended, zonal_speed, meridional, sea_local[None])
    flat_spectra = spectra.reshape(comp_local, cell_count)
    devices = comp_count * lat_count
    slice_len = cell_count // devices
    stride = 3 * slice_len // 4 // (lat_count - 1)
    sea_count = lat_count * (slice_len // 8) + stride * (lat_count * (lat_count - 1) // 2)
    dealt_slot = comp_place * lat_count + lat_place
    position_count = lat_count * slice_len
    received = lax.all_to_all(
        flat_spectra, ("comp", "lat"), split_axis=1, concat_axis=1, tiled=True
    )
    tile_flags = lax.dynamic_slice_in_dim(
        sea_mask.reshape(lat_count, cell_count), dealt_slot * slice_len, slice_len, 1
    ).reshape(-1)
    sea_index = jnp.nonzero(tile_flags, size=sea_count)[0].astype(jnp.int32)
    selector = (jnp.arange(position_count, dtype=jnp.int32)[:, None] == sea_index[None, :]).astype(
        jnp.float32
    )
    chosen_flat = jnp.dot(
        received.reshape(comp_local * comp_count, position_count),
        selector,
        precision=lax.Precision.HIGHEST,
        preferred_element_type=jnp.float32,
    )
    chosen = chosen_flat.reshape(comp_local, comp_count, sea_count)
    pair_in_blocks = pair_in.reshape(comp_count, comp_local, comp_count, comp_local)
    pair_out_blocks = pair_out.reshape(comp_count, comp_local, comp_count, comp_local)
    projected = jnp.einsum(
        "abcd,dcn->ban",
        pair_in_blocks,
        chosen.astype(jnp.bfloat16),
        preferred_element_type=jnp.float32,
    )
    pair_terms = (projected * chosen).astype(jnp.bfloat16)
    transfer = jnp.einsum(
        "abcd,dcn->ban", pair_out_blocks, pair_terms, preferred_element_type=jnp.float32
    )
    mean_energy = jnp.mean(chosen, axis=(0, 1), keepdims=True)
    wind_cols = wind_input.reshape(comp_count, comp_local).T[:, :, None]
    white_cols = whitecap.reshape(comp_count, comp_local).T[:, :, None]
    renewed = chosen + time_step * (
        wind_cols * chosen - white_cols * mean_energy * chosen + transfer
    )
    filled = jnp.dot(
        renewed.reshape(comp_local * comp_count, sea_count),
        selector.T,
        precision=lax.Precision.HIGHEST,
        preferred_element_type=jnp.float32,
    )
    returned = lax.all_to_all(
        filled.reshape(comp_local, devices * slice_len),
        ("comp", "lat"),
        split_axis=1,
        concat_axis=1,
        tiled=True,
    )
    return returned.reshape(comp_local, tile_rows, lon_cells)


def solution(mesh):
    placed = (P("comp", "lat", None), P(), P(), P(), P(), P(), P(), P())
    return jax.shard_map(
        per_device, mesh=mesh, in_specs=placed, out_specs=P("comp", "lat", None), check_vma=False
    )
```

profile of v0, /device:TPU:1, one launch (start us, length us, event | category | flops | bytes accessed | tf_op | source)
XLA Modules:
  0.0 346.4 jit_solution(15505944343509475617)
XLA Ops:
  0.0 0.9 fusion.37
  0.9 4.4 %copy_multiply_fusion = f32[225,4,1536]{2,0,1:T(8,128)S(1)} fusion(f32[225,4,1536]{2,1,0:T(4,128)} %param.8, f32[4,1536]{1,0:T(4,128)S(1)} %fusion.37), kind=kLoop, calls=%fused_computation.24 | loop fusion | flops 1382400 | bytes 11083776 | tf_op jit(solution)/shard_map/mul | solution.py:73
  5.3 2.5 copy-done
  7.8 1.8 fusion.53
  9.6 4.0 %collective-permute-start = (f32[225,1,1536]{2,0,1:T(8,128)}, f32[225,1,1536]{2,0,1:T(8,128)S(1)}, u32[]{:S(2)}, u32[]{:S(2)}) collective-permute-start(f32[225,1,1536]{2,0,1:T(8,128)} %get-tuple-element.23), channel_id=1, source_target_pairs={{0,1},{1,2},{2,3},{3,4},{4,5},{5,6},{6,7},{7,8},{8,9},{9,10},{10,1... | collective-permute-start | bytes 4147208 | tf_op jit(solution)/shard_map/ppermute | solution.py:22
  13.6 1.3 collective-permute-start.1
  14.9 0.7 fusion.46
  15.6 0.6 broadcast_compare_fusion.7
  16.2 0.1 copy.32
  16.3 0.7 gather_fusion
  17.0 1.2 slice_reduce_fusion.7
  18.3 10.3 %fusion.52 = (f32[225,4,1535]{2,0,1:T(8,128)}, f32[225,4,1535]{2,0,1:T(8,128)}) fusion(f32[225,4,1536]{2,0,1:T(8,128)} %copy-done), kind=kLoop, calls=%fused_computation.89 | loop fusion | bytes 22104000 | tf_op jit(solution)/shard_map/slice | solution.py:33
  28.5 15.2 %collective-permute-done = f32[225,1,1536]{2,0,1:T(8,128)S(1)} collective-permute-done((f32[225,1,1536]{2,0,1:T(8,128)}, f32[225,1,1536]{2,0,1:T(8,128)S(1)}, u32[]{:S(2)}, u32[]{:S(2)}) %collective-permute-start) | collective-permute-done | bytes 1382432 | tf_op jit(solution)/shard_map/ppermute | solution.py:22
  43.7 3.8 %collective-permute-done.1 = f32[225,1,1536]{2,0,1:T(8,128)S(1)} collective-permute-done((f32[225,1,1536]{2,0,1:T(8,128)}, f32[225,1,1536]{2,0,1:T(8,128)S(1)}, u32[]{:S(2)}, u32[]{:S(2)}) %collective-permute-start.1) | collective-permute-done | bytes 1382432 | tf_op jit(solution)/shard_map/ppermute | solution.py:23
  47.5 1.1 copy-done.4
  48.6 12.4 %fusion.14 = f32[225,4,1536]{2,0,1:T(8,128)S(1)} fusion(f32[225,4,1536]{2,0,1:T(8,128)S(1)} %bitcast.50, f32[225,1,1536]{2,0,1:T(8,128)} %copy-done.4, f32[225,1,1536]{2,0,1:T(8,128)} %copy-done.3, f32[225,4,1535]{2,0,1:T(8,128)} %get-tuple-element.22, f32[225,4,1535]{2,0,1:T(8,128)} %get-tuple-element.21, f32[225]{0:T(256)S(1)} %get-tuple-element.34, ...), kind=kLoop, calls=%fused_computation.19 | loop fusion | flops 49766400 | bytes 24958728 | tf_op jit(solution)/shard_map/mul | solution.py:45
  61.0 1.8 fusion.51
  62.7 4.2 %collective-permute-start.2 = (f32[225,1,1536]{2,0,1:T(8,128)}, f32[225,1,1536]{2,0,1:T(8,128)}, u32[]{:S(2)}, u32[]{:S(2)}) collective-permute-start(f32[225,1,1536]{2,0,1:T(8,128)} %get-tuple-element.19), channel_id=1, source_target_pairs={{0,1},{1,2},{2,3},{3,4},{4,5},{5,6},{6,7},{7,8},{8,9},{9,10},{10,1... | collective-permute-start | bytes 4147208 | tf_op jit(solution)/shard_map/ppermute | solution.py:22
  66.9 1.5 collective-permute-start.3
  68.4 4.5 %fusion.50 = (f32[225,4,1535]{2,0,1:T(8,128)S(1)}, f32[225,4,1535]{2,0,1:T(8,128)}) fusion(f32[225,4,1536]{2,0,1:T(8,128)S(1)} %fusion.14), kind=kLoop, calls=%fused_computation.87 | loop fusion | bytes 22104000 | tf_op jit(solution)/shard_map/slice | solution.py:33
  72.9 21.8 %collective-permute-done.2 = f32[225,1,1536]{2,0,1:T(8,128)} collective-permute-done((f32[225,1,1536]{2,0,1:T(8,128)}, f32[225,1,1536]{2,0,1:T(8,128)}, u32[]{:S(2)}, u32[]{:S(2)}) %collective-permute-start.2) | collective-permute-done | bytes 1382432 | tf_op jit(solution)/shard_map/ppermute | solution.py:22
  94.7 5.0 %collective-permute-done.3 = f32[225,1,1536]{2,0,1:T(8,128)} collective-permute-done((f32[225,1,1536]{2,0,1:T(8,128)}, f32[225,1,1536]{2,0,1:T(8,128)}, u32[]{:S(2)}, u32[]{:S(2)}) %collective-permute-start.3) | collective-permute-done | bytes 1382432 | tf_op jit(solution)/shard_map/ppermute | solution.py:23
  99.7 13.1 %fusion.7 = f32[225,4,1536]{2,0,1:T(8,128)} fusion(f32[225,4,1536]{2,0,1:T(8,128)S(1)} %fusion.14, f32[225,1,1536]{2,0,1:T(8,128)} %collective-permute-done.3, f32[225,1,1536]{2,0,1:T(8,128)} %collective-permute-done.2, f32[225,4,1535]{2,0,1:T(8,128)} %get-tuple-element.18, f32[225,4,1535]{2,0,1:T(8,128)S(1)} %get-tuple-element.17, ...), kind=kLoop, calls=%fused_computation.10 | loop fusion | flops 49766400 | bytes 24958728 | tf_op jit(solution)/shard_map/mul | solution.py:45
  112.8 6.4 %copy.33 = f32[225,4,1536]{0,2,1:T(8,128)} copy(f32[225,4,1536]{2,0,1:T(8,128)} %fusion.7) | data formatting | bytes 11059200 | tf_op jit(solution)/shard_map/mul | solution.py:45
  119.2 14.8 %all-to-all-start = ((f32[225,128,48]{0,2,1:T(8,128)}), f32[225,128,48]{0,2,1:T(8,128)}, u32[]{:S(2)}, u32[]{:S(2)}) async-start(f32[225,128,48]{0,2,1:T(8,128)} %bitcast.51), calls=%async_computation | async-start | bytes 12582912 | tf_op jit(solution)/shard_map/all_to_all | solution.py:92
  134.0 0.2 reshape.184
  134.2 0.7 fusion.48
  135.0 0.3 reduce-window.16
  135.3 0.1 slice.99
  135.4 0.1 slice_reduce_fusion.8
  135.6 6.1 %scatter_custom_fusion = s32[336]{0:T(512)S(1)} fusion(s32[768]{0:T(1024)S(1)} %fusion.39, s32[768]{0:T(1024)S(1)} %broadcast.199, s32[]{:T(128)} %constant.35.clone.1), kind=kCustom, calls=%fused_computation.82 | custom fusion | flops 768 | bytes 1348 | tf_op jit(solution)/shard_map/scatter-add | solution.py:98
  141.7 0.3 reduce-window.24
  142.1 16.7 %reshape.190 = bf16[8,225,8,225]{3,2,1,0:T(8,128)(2,1)} reshape(bf16[1800,1800]{1,0:T(8,128)(2,1)} %param.14) | data formatting | bytes 12960000 | tf_op jit(solution)/shard_map/reshape | solution.py:109
  158.8 16.7 %reshape.191 = bf16[8,225,8,225]{3,2,1,0:T(8,128)(2,1)} reshape(bf16[1800,1800]{1,0:T(8,128)(2,1)} %param.15) | data formatting | bytes 12960000 | tf_op jit(solution)/shard_map/reshape | solution.py:110
  175.5 0.1 reshape.188
  175.6 0.1 reshape.189
  175.7 0.1 slice_reduce_fusion.9
  175.9 0.7 fusion.40
  176.6 32.0 %all-to-all-done = f32[225,128,48]{0,2,1:T(8,128)} async-done(((f32[225,128,48]{0,2,1:T(8,128)}), f32[225,128,48]{0,2,1:T(8,128)}, u32[]{:S(2)}, u32[]{:S(2)}) %all-to-all-start) | async-done | bytes 5529632 | tf_op jit(solution)/shard_map/all_to_all | solution.py:92
  208.6 6.4 %fusion.54 = (f32[336]{0:T(512)S(1)}, f32[225,8,336]{0,2,1:T(8,128)S(1)}) fusion(f32[225,8,768]{0,2,1:T(8,128)} %bitcast.2, s32[336]{0:T(512)S(1)} %fusion.40), kind=kOutput, calls=%fused_computation.91 | convolution fusion | flops 5574699520 | bytes 7951488 | tf_op jit(solution)/shard_map/dot_general | solution.py:102
  215.0 3.1 fusion.27
  218.2 5.3 %fusion.21 = f32[225,8,336]{0,2,1:T(8,128)} fusion(f32[225,8,336]{0,2,1:T(8,128)S(1)} %get-tuple-element.33, bf16[225,8,336,1]{0,2,1,3:T(8,128)(2,1)S(1)} %fusion.27, bf16[8,225,8,225]{3,2,1,0:T(8,128)(2,1)S(1)} %bitcast.54, f32[336]{0:T(512)S(1)} %broadcast_multiply_fusion, f32[225,8]{0,1:T(8,128)S(1)} %bitcast.56, f32[225,8]{0,1:T(8,128)S(1)} %bitcast.55), kind=kOutput, calls=%fused_computation.31 | convolution fusion | flops 2181513216 | bytes 12543744 | tf_op jit(solution)/shard_map/abcd,dcn->ban/dot_general | solution.py:118
  223.5 2.7 copy.37
  226.2 6.9 %fusion.18 = f32[1800,768]{1,0:T(8,128)} fusion(f32[225,8,336]{2,1,0:T(8,128)S(1)} %copy.37, s32[336]{0:T(512)S(1)} %fusion.40), kind=kOutput, calls=%fused_computation.27 | convolution fusion | flops 5574094848 | bytes 7950144 | tf_op jit(solution)/shard_map/dot_general | solution.py:127
  233.2 12.5 %all_to_all.14 = f32[225,128,48]{2,1,0:T(8,128)} reshape(f32[1800,768]{1,0:T(8,128)} %fusion.18) | data formatting | bytes 11059200 | tf_op jit(solution)/shard_map/all_to_all | solution.py:133
  245.7 12.7 %copy.38 = f32[225,128,48]{0,2,1:T(8,128)} copy(f32[225,128,48]{2,1,0:T(8,128)} %all_to_all.14) | data formatting | bytes 11059200 | tf_op jit(solution)/shard_map/all_to_all | solution.py:133
  258.4 80.6 %all_to_all.18 = f32[225,128,48]{0,2,1:T(8,128)} all-to-all(f32[225,128,48]{0,2,1:T(8,128)} %copy.38), channel_id=1, replica_groups=mesh['comp'=8,'lat'=16] {'comp','lat'}, dimensions={1} | all-to-all | bytes 11059200 | tf_op jit(solution)/shard_map/all_to_all | solution.py:133
  339.0 7.4 %copy.39 = f32[225,4,1536]{2,1,0:T(4,128)} copy(f32[225,4,1536]{0,2,1:T(8,128)} %bitcast.52) | data formatting | bytes 11059200 | tf_op jit(solution)/shard_map/reshape | solution.py:140
  (39 shorter events, 0.5 us)
Async XLA Ops:
  0.9 14.7 %copy-start.5 = (s32[64,1536]{1,0:T(8,128)S(1)}, s32[64,1536]{1,0:T(8,128)}, u32[]{:S(2)}) copy-start(s32[64,1536]{1,0:T(8,128)} %param.10) | copy-start | bytes 1179652
  5.3 2.5 copy-start
  7.8 8.4 %copy-start.8 = (f32[50,8]{0,1:T(8,128)S(1)}, f32[50,8]{0,1:T(8,128)}, u32[]{:S(2)}) copy-start(f32[50,8]{0,1:T(8,128)} %param.11) | copy-start | bytes 4804
  9.6 34.1 %collective-permute-start = (f32[225,1,1536]{2,0,1:T(8,128)}, f32[225,1,1536]{2,0,1:T(8,128)S(1)}, u32[]{:S(2)}, u32[]{:S(2)}) collective-permute-start(f32[225,1,1536]{2,0,1:T(8,128)} %get-tuple-element.23), channel_id=1, source_target_pairs={{0,1},{1,2},{2,3},{3,4},{4,5},{5,6},{6,7},{7,8},{8,9},{9,10},{10,1... | collective-permute-start | bytes 4147208 | tf_op jit(solution)/shard_map/ppermute | solution.py:22
  13.6 33.9 %collective-permute-start.1 = (f32[225,1,1536]{2,0,1:T(8,128)}, f32[225,1,1536]{2,0,1:T(8,128)S(1)}, u32[]{:S(2)}, u32[]{:S(2)}) collective-permute-start(f32[225,1,1536]{2,0,1:T(8,128)} %get-tuple-element.24), channel_id=1, source_target_pairs={{1,0},{2,1},{3,2},{4,3},{5,4},{6,5},{7,6},{8,7},{9,8},{10,9},{11,1... | collective-permute-start | bytes 4147208 | tf_op jit(solution)/shard_map/ppermute | solution.py:23
  17.0 31.6 %slice-start = ((s8[5701632]{0:T(1024)(128)(4,1)}), s8[4194304]{0:T(1024)(128)(4,1)S(1)}, s32[]{:S(2)}) async-start(s8[5701632]{0:T(1024)(128)(4,1)} %bitcast.49), calls=%async_computation.2 | async-start | bytes 8388608
  18.3 30.3 %slice-start.1 = ((s8[5701632]{0:T(1024)(128)(4,1)}), s8[1507328]{0:T(1024)(128)(4,1)S(1)}, s32[]{:S(2)}) async-start(s8[5701632]{0:T(1024)(128)(4,1)} %bitcast.49), calls=%async_computation.3 | async-start | bytes 3014656
  43.7 3.8 %copy-start.3 = (f32[225,1,1536]{2,0,1:T(8,128)}, f32[225,1,1536]{2,0,1:T(8,128)S(1)}, u32[]{:S(2)}) copy-start(f32[225,1,1536]{2,0,1:T(8,128)S(1)} %collective-permute-done) | copy-start | bytes 4147204
  47.5 1.1 copy-start.4
  62.7 32.0 %collective-permute-start.2 = (f32[225,1,1536]{2,0,1:T(8,128)}, f32[225,1,1536]{2,0,1:T(8,128)}, u32[]{:S(2)}, u32[]{:S(2)}) collective-permute-start(f32[225,1,1536]{2,0,1:T(8,128)} %get-tuple-element.19), channel_id=1, source_target_pairs={{0,1},{1,2},{2,3},{3,4},{4,5},{5,6},{6,7},{7,8},{8,9},{9,10},{10,1... | collective-permute-start | bytes 4147208 | tf_op jit(solution)/shard_map/ppermute | solution.py:22
  66.9 32.8 %collective-permute-start.3 = (f32[225,1,1536]{2,0,1:T(8,128)}, f32[225,1,1536]{2,0,1:T(8,128)}, u32[]{:S(2)}, u32[]{:S(2)}) collective-permute-start(f32[225,1,1536]{2,0,1:T(8,128)} %get-tuple-element.20), channel_id=1, source_target_pairs={{1,0},{2,1},{3,2},{4,3},{5,4},{6,5},{7,6},{8,7},{9,8},{10,9},{11,1... | collective-permute-start | bytes 4147208 | tf_op jit(solution)/shard_map/ppermute | solution.py:23
  119.2 14.8 %copy-start.2 = (s32[64,1536]{1,0:T(8,128)S(1)}, s32[64,1536]{1,0:T(8,128)}, u32[]{:S(2)}) copy-start(s32[64,1536]{1,0:T(8,128)} %param.9) | copy-start | bytes 1179652
  119.2 89.4 %all-to-all-start = ((f32[225,128,48]{0,2,1:T(8,128)}), f32[225,128,48]{0,2,1:T(8,128)}, u32[]{:S(2)}, u32[]{:S(2)}) async-start(f32[225,128,48]{0,2,1:T(8,128)} %bitcast.51), calls=%async_computation | async-start | bytes 12582912 | tf_op jit(solution)/shard_map/all_to_all | solution.py:92
  158.8 16.7 %copy-start.6 = (f32[1800]{0:T(1024)S(1)}, f32[1800]{0:T(1024)}, u32[]{:S(2)}) copy-start(f32[1800]{0:T(1024)} %param.12) | copy-start | bytes 21604
  158.8 16.8 %copy-start.7 = (f32[1800]{0:T(1024)S(1)}, f32[1800]{0:T(1024)}, u32[]{:S(2)}) copy-start(f32[1800]{0:T(1024)} %param.13) | copy-start | bytes 21604
  208.6 6.4 %copy-start.1 = (bf16[8,225,8,225]{3,2,1,0:T(8,128)(2,1)S(1)}, bf16[8,225,8,225]{3,2,1,0:T(8,128)(2,1)}, u32[]{:S(2)}) copy-start(bf16[8,225,8,225]{3,2,1,0:T(8,128)(2,1)} %reshape.190) | copy-start | bytes 19440004
  208.6 9.5 %slice-start.2 = ((s8[7372800]{0:T(1024)(128)(4,1)}), s8[4194304]{0:T(1024)(128)(4,1)S(1)}, s32[]{:S(2)}) async-start(s8[7372800]{0:T(1024)(128)(4,1)} %bitcast.53), calls=%async_computation.4 | async-start | bytes 8388608
  215.0 3.1 slice-start.3
where the time goes:
time: 348 us; the launch traced here: 346 us
  local copies, waits for them, and re-layouts  99.8 us (29%)
  blocking collectives  80.6 us (23%)
  waiting for transfers between devices  77.8 us (22%)
  other arithmetic  40.4 us (12%)
  starting transfers between devices  25.7 us (7%)
  matrix products  21.8 us (6%)
    all_to_all x1, blocking collectives, per_device(): lax.all_to_all(filled.reshape(comp_local, devices * slice_len), ('comp',...  80.6 us
    ppermute x2, waiting for transfers between devices, extended_2(): before = lax.ppermute(last, axis, up)  37 us
    all_to_all x1, waiting for transfers between devices, per_device(): lax.all_to_all(flat_spectra, ('comp', 'lat'), split_axis=1, concat_axis=1...  32 us
    mul x2, other arithmetic, upwind(): return advected * sea_cells  25.5 us
    all_to_all x2, local copies, waits for them, and re-layouts, per_device(): lax.all_to_all(filled.reshape(comp_local, devices * slice_len), ('comp',...  25.2 us
    reshape x1, local copies, waits for them, and re-layouts, per_device(): pair_out.reshape(comp_count, comp_local, comp_count, comp_local)  16.7 us
    reshape x1, local copies, waits for them, and re-layouts, per_device(): pair_in.reshape(comp_count, comp_local, comp_count, comp_local)  16.7 us
    all_to_all x1, starting transfers between devices, per_device(): lax.all_to_all(flat_spectra, ('comp', 'lat'), split_axis=1, concat_axis=1...  14.8 us
  transfers between devices with their start and end apart: 5, of which 5 were waited for; matrix products, arithmetic and copies ran while one was open for 17% of the time, Pallas kernels for 0%

commit v1 on v0

v1 whole, which is shorter than its diff:
```python
import math

import jax
import jax.numpy as jnp
from jax import lax
from jax.experimental import pallas as pl
from jax.experimental.pallas import tpu as pltpu
from jax.sharding import PartitionSpec as P

NDIR = 36
SUB = 2
MESH = pl.DeviceIdType.MESH
F32 = jnp.float32
BF16 = jnp.bfloat16

time_step = 0.5

LANE = 128
CHUNK = 256
RUN = 18


def sections(lon):
    tiles, step = lon // LANE, CHUNK // LANE
    ends = [0] + [min(step * (q + 1) + 1, tiles) for q in range(lon // CHUNK)]
    return [(low, high - low) for low, high in zip(ends, ends[1:])]


def make_kernel(comp_count, lat_count, comp_local, rows, lon):
    chunks = lon // CHUNK
    total = comp_count * comp_local
    parts = sections(lon)
    window = CHUNK + 2 * LANE
    groups = comp_local // 8
    runs = comp_local // RUN
    rest = comp_local - runs * RUN
    row_tiles = [(0, 448), (448, 448), (896, 448), (1344, total - 1344)]

    def kernel(
        energy,
        pair_in,
        pair_out,
        sea,
        classes,
        table,
        rates,
        out,
        cells,
        halo,
        advected,
        gathered,
        returned,
        map_in,
        map_out,
        half,
        terms,
        load_sem,
        map_sem,
        halo_send,
        halo_recv,
        there_send,
        there_recv,
        back_send,
        back_recv,
        out_sem,
    ):
        c = lax.axis_index("comp")
        l = lax.axis_index("lat")
        odd = lax.rem(c, 2)

        def own(low, size):
            return pl.ds(low + 1, size)

        for q, (low, size) in enumerate(parts):
            for tile in range(low, low + size):
                for r in range(rows):
                    pltpu.make_async_copy(
                        energy.at[:, r, pl.ds(tile * LANE, LANE)],
                        cells.at[tile + 1, r],
                        load_sem.at[q],
                    ).start()

        barrier = pltpu.get_barrier_semaphore()
        north = lax.rem(l + 1, lat_count)
        south = lax.rem(l + lat_count - 1, lat_count)
        for d in range(1, comp_count):
            pl.semaphore_signal(
                barrier, inc=1, device_id=(lax.rem(c + d, comp_count), l), device_id_type=MESH
            )
        for other in (north, south):
            pl.semaphore_signal(barrier, inc=1, device_id=(c, other), device_id_type=MESH)
        pl.semaphore_wait(barrier, comp_count + 1)

        def send_halo(start, count, up, q):
            low, size = parts[q]
            for near in range(2):
                for is_up in (True, False):

                    @pl.when(up if is_up else jnp.logical_not(up))
                    def _():
                        pltpu.make_async_remote_copy(
                            src_ref=cells.at[
                                own(low, size),
                                rows - 1 - near if is_up else near,
                                pl.ds(start, count),
                            ],
                            dst_ref=halo.at[own(low, size), near, pl.ds(start, count)],
                            send_sem=halo_send.at[q],
                            recv_sem=halo_recv.at[q],
                            device_id=(c, north if is_up else south),
                            device_id_type=MESH,
                        ).start()

        for q, (low, size) in enumerate(parts):
            part = cells.at[own(low, size)]
            pltpu.make_async_copy(part, part, load_sem.at[q]).wait()

            @pl.loop(0, runs)
            def _(m):
                up = lax.rem((c + odd) // 2 + m, 2) == 0
                send_halo(m * RUN + odd * rest, RUN, up, q)

            send_halo((1 - odd) * runs * RUN, rest, lax.rem(c, 4) < 2, q)

        pltpu.make_async_copy(pair_in, map_in, map_sem.at[0]).start()
        pltpu.make_async_copy(pair_out, map_out, map_sem.at[1]).start()

        def advect_group(q, start):
            here = pl.ds(start, 8)
            lanes = pl.ds(pl.multiple_of(q * CHUNK, LANE), window)
            wide = (8, window)
            facts = table[here, :]
            tile = q * (CHUNK // LANE)

            def strip(ref, i):
                return jnp.concatenate(
                    [ref[tile + t, i, here, :] for t in range(window // LANE)], axis=1
                )

            def column(j):
                return jnp.broadcast_to(facts[:, j : j + 1], wide)

            cosine, sine = column(8), column(9)
            up = sine > 0.0
            eastward = cosine > 0.0

            def sea_row(i):
                return jnp.broadcast_to(sea[pl.ds(i, 1), lanes], wide)

            def class_row(i):
                return jnp.broadcast_to(classes[pl.ds(i, 1), lanes], wide)

            speeds = [column(j) for j in range(8)]

            def rates_of(kinds):
                speed = speeds[0]
                for level in range(1, 8):
                    speed = jnp.where(kinds == level, speeds[level], speed)
                return jnp.abs(speed * cosine), jnp.abs(speed * sine)

            def beside(v):
                return jnp.where(eastward, pltpu.roll(v, 1, 1), pltpu.roll(v, window - 1, 1))

            def moved(v, along, across, zonal, meridional, wet):
                return (v - zonal * (v - along) - meridional * (v - across)) * wet

            wet = [sea_row(i + 2) for i in range(rows)]
            wet_near = jnp.where(up, sea_row(1), sea_row(6))
            wet_far = jnp.where(up, sea_row(0), sea_row(7))
            e = [jnp.where(wet[i] > 0.0, strip(cells, i), 0.0) for i in range(rows)]
            near = jnp.where(wet_near > 0.0, strip(halo, 0), 0.0)
            far = jnp.where(wet_far > 0.0, strip(halo, 1), 0.0)
            speed_of = [rates_of(class_row(i + 2)) for i in range(rows)]
            near_speed = rates_of(jnp.where(up, class_row(1), class_row(6)))

            def across(v, edge, i):
                before = edge if i == 0 else v[i - 1]
                after = edge if i == rows - 1 else v[i + 1]
                return jnp.where(up, before, after)

            first = [
                moved(e[i], beside(e[i]), across(e, near, i), *speed_of[i], wet[i])
                for i in range(rows)
            ]
            first_near = moved(near, beside(near), far, *near_speed, wet_near)
            for i in range(rows):
                second = moved(
                    first[i], beside(first[i]), across(first, first_near, i), *speed_of[i], wet[i]
                )
                for t in range(CHUNK // LANE):
                    advected[q * comp_count + i * 2 + t, here, :] = second[
                        :, LANE * (t + 1) : LANE * (t + 2)
                    ]

        def wait_part(q):
            for k, (low, size) in enumerate(parts):

                @pl.when(q == k)
                def _():
                    part = halo.at[own(low, size)]
                    pltpu.make_async_copy(part, part, halo_recv.at[k]).wait()

        @pl.loop(0, chunks)
        def _(q):
            wait_part(q)

            @pl.loop(0, groups)
            def _(g):
                advect_group(q, pl.multiple_of(g * 8, 8))

            advect_group(q, comp_local - 8)

            place = gathered.at[q, pl.ds(c * comp_local, comp_local)]
            pltpu.make_async_copy(advected.at[q * comp_count + c], place, there_recv.at[q]).start()

            @pl.loop(1, comp_count)
            def _(d):
                home = lax.rem(c + d, comp_count)
                pltpu.make_async_remote_copy(
                    src_ref=advected.at[q * comp_count + home],
                    dst_ref=place,
                    send_sem=there_send.at[q],
                    recv_sem=there_recv.at[q],
                    device_id=(home, l),
                    device_id_type=MESH,
                ).start()

        pltpu.make_async_copy(pair_in, map_in, map_sem.at[0]).wait()
        pltpu.make_async_copy(pair_out, map_out, map_sem.at[1]).wait()

        @pl.loop(0, chunks)
        def _(q):
            pltpu.make_async_copy(gathered.at[q], gathered.at[q], there_recv.at[q]).wait()
            spectra = gathered[q]
            half[...] = spectra.astype(BF16)
            mean_energy = jnp.sum(spectra, axis=0, keepdims=True) * (1.0 / total)
            for low, size in row_tiles:
                projected = jnp.dot(
                    map_in[low : low + size, :], half[...], preferred_element_type=F32
                )
                terms[low : low + size, :] = (
                    projected * gathered[q, low : low + size, :]
                ).astype(BF16)
            for low, size in row_tiles:
                transfer = jnp.dot(
                    map_out[low : low + size, :], terms[...], preferred_element_type=F32
                )
                now = gathered[q, low : low + size, :]
                wind = rates[low : low + size, 0:1]
                white = rates[low : low + size, 1:2]
                gathered[q, low : low + size, :] = now + time_step * (
                    wind * now - white * mean_energy * now + transfer
                )

            place = returned.at[q * comp_count + c]
            pltpu.make_async_copy(
                gathered.at[q, pl.ds(c * comp_local, comp_local)], place, back_recv.at[q]
            ).start()

            @pl.loop(1, comp_count)
            def _(d):
                origin = lax.rem(c + d, comp_count)
                pltpu.make_async_remote_copy(
                    src_ref=gathered.at[q, pl.ds(origin * comp_local, comp_local)],
                    dst_ref=place,
                    send_sem=back_send.at[q],
                    recv_sem=back_recv.at[q],
                    device_id=(origin, l),
                    device_id_type=MESH,
                ).start()

        def write(q, i, t):
            b = q * comp_count + i * 2 + t
            return pltpu.make_async_copy(
                returned.at[b], out.at[:, i, pl.ds(q * CHUNK + t * LANE, LANE)], out_sem.at[b]
            )

        for q in range(chunks):
            pltpu.make_async_copy(gathered.at[q], gathered.at[q], back_recv.at[q]).wait()
            for i in range(rows):
                for t in range(CHUNK // LANE):
                    write(q, i, t).start()

        sent = gathered.at[0, pl.ds(0, (comp_count - 1) * comp_local)]
        for q, (low, size) in enumerate(parts):
            pltpu.make_async_copy(sent, sent, there_send.at[q]).wait()
            pltpu.make_async_copy(sent, sent, back_send.at[q]).wait()
            part = halo.at[own(low, size)]
            pltpu.make_async_copy(part, part, halo_send.at[q]).wait()
        for q in range(chunks):
            for i in range(rows):
                for t in range(CHUNK // LANE):
                    write(q, i, t).wait()

    return kernel


def per_device(energy, sea_mask, depth_class, group_speed, wind_input, whitecap, pair_in, pair_out):
    comp_count = lax.axis_size("comp")
    lat_count = lax.axis_size("lat")
    comp_local, rows, lon = energy.shape
    total = comp_local * comp_count
    chunks = lon // CHUNK
    lat_place = lax.axis_index("lat")
    comp_place = lax.axis_index("comp")
    comp_ids = comp_place * comp_local + jnp.arange(comp_local)
    angles = 2.0 * math.pi * ((comp_ids % NDIR).astype(F32) + 0.5) / NDIR
    speed_table = lax.dynamic_slice_in_dim(
        jnp.repeat(group_speed, NDIR, axis=0), comp_place * comp_local, comp_local, 0
    )
    table = jnp.concatenate(
        [speed_table, jnp.cos(angles)[:, None], jnp.sin(angles)[:, None]], axis=1
    )
    rates = jnp.stack([wind_input, whitecap], axis=1)

    def band(x):
        x = jnp.pad(x, ((SUB, SUB), (LANE, LANE)))
        return lax.dynamic_slice_in_dim(x, lat_place * rows, rows + 2 * SUB, 0)

    sea = band(sea_mask).astype(F32)
    classes = band(depth_class)
    blocks = chunks * comp_count
    anywhere = pl.BlockSpec(memory_space=pl.ANY)
    near = pl.BlockSpec(memory_space=pltpu.VMEM)
    dma = pltpu.SemaphoreType.DMA
    return pl.pallas_call(
        make_kernel(comp_count, lat_count, comp_local, rows, lon),
        out_shape=jax.ShapeDtypeStruct(energy.shape, F32),
        in_specs=[anywhere] * 3 + [near] * 4,
        out_specs=anywhere,
        scratch_shapes=[
            pltpu.VMEM((lon // LANE + 2, rows, comp_local, LANE), F32),
            pltpu.VMEM((lon // LANE + 2, 2, comp_local, LANE), F32),
            pltpu.VMEM((blocks, comp_local, LANE), F32),
            pltpu.VMEM((chunks, total, LANE), F32),
            pltpu.VMEM((blocks, comp_local, LANE), F32),
            pltpu.VMEM((total, total), BF16),
            pltpu.VMEM((total, total), BF16),
            pltpu.VMEM((total, LANE), BF16),
            pltpu.VMEM((total, LANE), BF16),
            dma((chunks,)),
            dma((2,)),
            dma((chunks,)),
            dma((chunks,)),
            dma((chunks,)),
            dma((chunks,)),
            dma((chunks,)),
            dma((chunks,)),
            dma((blocks,)),
        ],
        compiler_params=pltpu.CompilerParams(
            collective_id=0, has_side_effects=True, vmem_limit_bytes=58 * 2**20
        ),
        cost_estimate=pl.CostEstimate(
            flops=4 * total * total * chunks * LANE, bytes_accessed=24 * 2**20, transcendentals=0
        ),
    )(energy, pair_in, pair_out, sea, classes, table, rates)


def solution(mesh):
    placed = (P("comp", "lat", None), P(), P(), P(), P(), P(), P(), P())
    return jax.shard_map(
        per_device, mesh=mesh, in_specs=placed, out_specs=P("comp", "lat", None), check_vma=False
    )
```

time: 348 us -> 162 us (0.47)
  Pallas kernels: 0 us -> 149 us
  local copies, waits for them, and re-layouts: 99.8 us -> 10.4 us
  blocking collectives: 80.6 us -> 0 us
  waiting for transfers between devices: 77.8 us -> 0 us
  other arithmetic: 40.4 us -> 1.7 us
  starting transfers between devices: 25.7 us -> 0 us
  matrix products: 21.8 us -> 0 us
    pallas_call x0 -> x1, Pallas kernels: none -> 149 us  [per_device(): pl.pallas_call(make_kernel(comp_count, lat_count, comp_local, rows, lon),...]
    all_to_all x1 -> x0, blocking collectives: 80.6 us -> none  [per_device(): lax.all_to_all(filled.reshape(comp_local, devices * slice_len), ('comp',...]
    ppermute x4 -> x0, waiting for transfers between devices: 45.8 us -> none  [the longest x2 37 us: extended_2(): before = lax.ppermute(last, axis, up)]
    reshape x6 -> x1, local copies, waits for them, and re-layouts: 41.1 us -> 0.12 us  [per_device(): jnp.repeat(group_speed, NDIR, axis=0)]
    all_to_all x1 -> x0, waiting for transfers between devices: 32 us -> none  [per_device(): lax.all_to_all(flat_spectra, ('comp', 'lat'), split_axis=1, concat_axis=1...]
    mul x3 -> x0, other arithmetic: 29.9 us -> none  [the longest x2 25.5 us: upwind(): return advected * sea_cells]
    all_to_all x2 -> x0, local copies, waits for them, and re-layouts: 25.2 us -> none  [per_device(): lax.all_to_all(filled.reshape(comp_local, devices * slice_len), ('comp',...]
    dot_general x4 -> x0, matrix products: 21.8 us -> none  [the longest x1 6.93 us: per_device(): jnp.dot(renewed.reshape(comp_local * comp_count, sea_count), selector.T,...]
  transfers between devices with their start and end apart: 5 -> 0, of which waited for: 5 -> 0; matrix products, arithmetic and copies ran while one was open for 17% -> 0% of each run, Pallas kernels for 0% -> 0%
where the time goes in v1:
time: 162 us; the launch traced here: 161 us
  Pallas kernels  149 us (92%)
  local copies, waits for them, and re-layouts  10.4 us (6%)
  other arithmetic  1.7 us (1%)
    pallas_call x1, Pallas kernels, per_device(): pl.pallas_call(make_kernel(comp_count, lat_count, comp_local, rows, lon),...  149 us
    unnamed x1, local copies, waits for them, and re-layouts  5.97 us

profile of v1, /device:TPU:1, one launch (start us, length us, event | category | flops | bytes accessed | tf_op | source)
XLA Modules:
  0.0 161.3 jit_solution(3836141809904569201)
XLA Ops:
  0.0 0.1 fusion.4
  0.1 0.7 stack.9
  0.8 0.7 stack.10
  1.5 1.6 pad_dynamic-slice_fusion
  3.1 0.8 broadcast_in_dim.2
  3.9 0.1 reshape.44
  4.0 0.1 constant_dynamic-slice_fusion
  4.1 0.8 copy.13.table
  4.9 1.3 copy.14.rates
  6.2 149.2 %shard_map.82 = f32[225,4,1536]{2,1,0:T(4,128)} custom-call(f32[225,4,1536]{2,1,0:T(4,128)} %energy.1, bf16[1800,1800]{1,0:T(8,128)(2,1)} %pair_in.1, bf16[1800,1800]{1,0:T(8,128)(2,1)} %pair_out.1, f32[8,1792]{1,0:T(8,128)} %get-tuple-element.8.sea, s32[8,1792]{1,0:T(8,128)} %get-tuple-element.7.classes, f32[225,10]{1,0:T(8,128)} %copy.13.table, ...), custom_call_target="tpu_custom_call" | custom-call | flops 9953280000 | bytes 25165824 | tf_op jit(solution)/shard_map/pallas_call | solution.py:326
  155.3 6.0 %copy.16 = f32[225,4,1536]{2,1,0:T(4,128)} copy(f32[225,4,1536]{2,1,0:T(4,128)} %shard_map.82) | data formatting | bytes 11059200
  (2 shorter events, 0.0 us)

commit v2 on v1

--- a/solution.py
+++ b/solution.py
@@ -1,6 +1,7 @@
 import math
 
 import jax
+import numpy as np
 import jax.numpy as jnp
 from jax import lax
 from jax.experimental import pallas as pl
@@ -18,6 +19,8 @@
 LANE = 128
 CHUNK = 256
 RUN = 18
+EARLY = 3
+PAIR = 2
 
 
 def sections(lon):
@@ -30,23 +33,29 @@
     chunks = lon // CHUNK
     total = comp_count * comp_local
     parts = sections(lon)
-    window = CHUNK + 2 * LANE
+    tiles = lon // LANE
+    spread = CHUNK // LANE + 1
+    window = spread * LANE
     groups = comp_local // 8
     runs = comp_local // RUN
     rest = comp_local - runs * RUN
+    quarter = runs // 4
+    tail_groups = [*range(groups // PAIR * PAIR * 8, comp_local - 7, 8), comp_local - 8]
     row_tiles = [(0, 448), (448, 448), (896, 448), (1344, total - 1344)]
 
     def kernel(
         energy,
         pair_in,
         pair_out,
-        sea,
-        classes,
-        table,
-        rates,
+        sea_mask,
+        depth_class,
+        group_speed,
+        wind_input,
+        whitecap,
         out,
         cells,
         halo,
+        early,
         advected,
         gathered,
         returned,
@@ -54,7 +63,15 @@
         map_out,
         half,
         terms,
+        mask_rows,
+        class_rows,
+        sea,
+        classes,
+        rates_rows,
+        rates,
+        trig,
         load_sem,
+        fact_sem,
         map_sem,
         halo_send,
         halo_recv,
@@ -71,7 +88,8 @@
         def own(low, size):
             return pl.ds(low + 1, size)
 
-        for q, (low, size) in enumerate(parts):
+        def load_cells(q):
+            low, size = parts[q]
             for tile in range(low, low + size):
                 for r in range(rows):
                     pltpu.make_async_copy(
@@ -79,6 +97,23 @@
                         cells.at[tile + 1, r],
                         load_sem.at[q],
                     ).start()
+
+        def wait_cells(q):
+            low, size = parts[q]
+            part = cells.at[own(low, size)]
+            pltpu.make_async_copy(part, part, load_sem.at[q]).wait()
+
+        lat_rows = lat_count * rows
+        fact_low = jnp.clip((l * rows - SUB + 8) // 8 - 1, 0, lat_rows // 8 - 2) * 8
+        fact_rows = pl.ds(pl.multiple_of(fact_low, 8), 16)
+        fact_copies = [
+            pltpu.make_async_copy(sea_mask.at[fact_rows], mask_rows, fact_sem.at[0]),
+            pltpu.make_async_copy(depth_class.at[fact_rows], class_rows, fact_sem.at[1]),
+        ]
+        for copy in fact_copies:
+            copy.start()
+        for q in range(chunks):
+            load_cells(q)
 
         barrier = pltpu.get_barrier_semaphore()
         north = lax.rem(l + 1, lat_count)
@@ -89,7 +124,38 @@
             )
         for other in (north, south):
             pl.semaphore_signal(barrier, inc=1, device_id=(c, other), device_id_type=MESH)
-        pl.semaphore_wait(barrier, comp_count + 1)
+
+        angles = 2.0 * math.pi * (np.arange(trig.shape[1]) % NDIR + 0.5) / NDIR
+        for i, values in enumerate((np.cos(angles), np.sin(angles))):
+            for j, value in enumerate(values):
+                trig[i, j : j + 1, :] = jnp.full((1, LANE), value, F32)
+
+        lane = lax.broadcasted_iota(jnp.int32, (8, LANE), 1)
+
+        def edge(before, after):
+            return jnp.where(lane < LANE // 2, after, before)
+
+        for copy in fact_copies:
+            copy.wait()
+        for i in range(rows + 2 * SUB):
+            row = l * rows + i - SUB
+            inside = jnp.logical_and(row >= 0, row < lat_rows).astype(jnp.int32)
+            at = pl.ds(jnp.clip(row, 0, lat_rows - 1) - fact_low, 1)
+            for ref, values in (
+                (sea, (mask_rows[at, :] * inside).astype(F32)),
+                (classes, class_rows[at, :]),
+            ):
+                blank = jnp.zeros((8, LANE), values.dtype)
+                wide = [
+                    jnp.broadcast_to(values[:, k * LANE : (k + 1) * LANE], (8, LANE))
+                    for k in range(tiles)
+                ]
+                wide = [blank] + wide + [blank]
+                for q in range(chunks):
+                    first = q * (CHUNK // LANE)
+                    for t in range(spread - 1):
+                        ref[i, q * spread + t] = wide[first + 1 + t]
+                    ref[i, q * spread + spread - 1] = edge(wide[first], wide[first + spread])
 
         def send_halo(start, count, up, q):
             low, size = parts[q]
@@ -111,48 +177,71 @@
                             device_id_type=MESH,
                         ).start()
 
-        for q, (low, size) in enumerate(parts):
-            part = cells.at[own(low, size)]
-            pltpu.make_async_copy(part, part, load_sem.at[q]).wait()
+        def run_of(m):
+            return m * RUN + odd * rest, lax.rem((c + odd) // 2 + m, 2) == 0
+
+        rest_run = ((1 - odd) * runs * RUN, lax.rem(c, 4) < 2)
+
+        def send_halos(q):
+            if q >= EARLY:
+                wait_cells(q)
 
             @pl.loop(0, runs)
             def _(m):
-                up = lax.rem((c + odd) // 2 + m, 2) == 0
-                send_halo(m * RUN + odd * rest, RUN, up, q)
-
-            send_halo((1 - odd) * runs * RUN, rest, lax.rem(c, 4) < 2, q)
-
-        pltpu.make_async_copy(pair_in, map_in, map_sem.at[0]).start()
-        pltpu.make_async_copy(pair_out, map_out, map_sem.at[1]).start()
-
-        def advect_group(q, start):
+                start, up = run_of(m)
+                send_halo(start, RUN, up, q)
+
+            send_halo(rest_run[0], rest, rest_run[1], q)
+
+        def meet():
+            pl.semaphore_wait(barrier, comp_count + 1)
+
+        def after_first():
+            for q in range(EARLY):
+                send_halos(q)
+
+        def advect_group(q, start, wanted, put):
             here = pl.ds(start, 8)
-            lanes = pl.ds(pl.multiple_of(q * CHUNK, LANE), window)
-            wide = (8, window)
-            facts = table[here, :]
             tile = q * (CHUNK // LANE)
-
-            def strip(ref, i):
-                return jnp.concatenate(
-                    [ref[tile + t, i, here, :] for t in range(window // LANE)], axis=1
-                )
-
-            def column(j):
-                return jnp.broadcast_to(facts[:, j : j + 1], wide)
-
-            cosine, sine = column(8), column(9)
+            ident = c * comp_local + start
+            first_tile = q * spread
+            sublane = lax.broadcasted_iota(jnp.int32, (8, LANE), 0)
+            low_freq = ident // NDIR
+            high_freq = (ident + 7) // NDIR
+            later = sublane + lax.rem(ident, NDIR) >= NDIR
+
+            def wide(v):
+                return jnp.concatenate([v] * spread, axis=1)
+
+            angle = pl.ds(lax.rem(ident, NDIR), 8)
+            cosine, sine = wide(trig[0, angle, :]), wide(trig[1, angle, :])
             up = sine > 0.0
             eastward = cosine > 0.0
-
-            def sea_row(i):
-                return jnp.broadcast_to(sea[pl.ds(i, 1), lanes], wide)
-
-            def class_row(i):
-                return jnp.broadcast_to(classes[pl.ds(i, 1), lanes], wide)
-
-            speeds = [column(j) for j in range(8)]
-
-            def rates_of(kinds):
+            speeds = [
+                wide(jnp.where(later, group_speed[j, high_freq], group_speed[j, low_freq]))
+                for j in range(8)
+            ]
+
+            def strip(ref, i):
+                parts = [ref[tile + t, i, here, :] for t in range(spread + 1)]
+                return jnp.concatenate(parts[1:-1] + [edge(parts[0], parts[-1])], axis=1)
+
+            def fact(ref, i):
+                return jnp.concatenate([ref[i, first_tile + t] for t in range(spread)], axis=1)
+
+            def facing(ref, i):
+                return jnp.where(up, fact(ref, i + SUB), fact(ref, SUB + rows - 1 - i))
+
+            def upstream(i):
+                wet = facing(sea, i)
+                if i < 0:
+                    value = strip(halo, -1 - i)
+                else:
+                    value = jnp.where(up, strip(cells, i), strip(cells, rows - 1 - i))
+                return jnp.where(wet > 0.0, value, 0.0), wet
+
+            def rates_of(i):
+                kinds = facing(classes, i)
                 speed = speeds[0]
                 for level in range(1, 8):
                     speed = jnp.where(kinds == level, speeds[level], speed)
@@ -161,36 +250,21 @@
             def beside(v):
                 return jnp.where(eastward, pltpu.roll(v, 1, 1), pltpu.roll(v, window - 1, 1))
 
-            def moved(v, along, across, zonal, meridional, wet):
-                return (v - zonal * (v - along) - meridional * (v - across)) * wet
-
-            wet = [sea_row(i + 2) for i in range(rows)]
-            wet_near = jnp.where(up, sea_row(1), sea_row(6))
-            wet_far = jnp.where(up, sea_row(0), sea_row(7))
-            e = [jnp.where(wet[i] > 0.0, strip(cells, i), 0.0) for i in range(rows)]
-            near = jnp.where(wet_near > 0.0, strip(halo, 0), 0.0)
-            far = jnp.where(wet_far > 0.0, strip(halo, 1), 0.0)
-            speed_of = [rates_of(class_row(i + 2)) for i in range(rows)]
-            near_speed = rates_of(jnp.where(up, class_row(1), class_row(6)))
-
-            def across(v, edge, i):
-                before = edge if i == 0 else v[i - 1]
-                after = edge if i == rows - 1 else v[i + 1]
-                return jnp.where(up, before, after)
-
-            first = [
-                moved(e[i], beside(e[i]), across(e, near, i), *speed_of[i], wet[i])
-                for i in range(rows)
-            ]
-            first_near = moved(near, beside(near), far, *near_speed, wet_near)
-            for i in range(rows):
-                second = moved(
-                    first[i], beside(first[i]), across(first, first_near, i), *speed_of[i], wet[i]
-                )
-                for t in range(CHUNK // LANE):
-                    advected[q * comp_count + i * 2 + t, here, :] = second[
-                        :, LANE * (t + 1) : LANE * (t + 2)
-                    ]
+            def moved(v, across, zonal, meridional, wet):
+                return (v - zonal * (v - beside(v)) - meridional * (v - across)) * wet
+
+            behind, _ = upstream(wanted[0] - 2)
+            earlier = None
+            for i in range(wanted[0] - 1, wanted[-1] + 1):
+                value, wet = upstream(i)
+                speed = rates_of(i)
+                first = moved(value, behind, *speed, wet)
+                behind = value
+                if i >= wanted[0]:
+                    second = moved(first, earlier, *speed, wet)
+                    for t in range(CHUNK // LANE):
+                        put(i, t, here, second[:, LANE * t : LANE * (t + 1)], up[:, :LANE])
+                earlier = first
 
         def wait_part(q):
             for k, (low, size) in enumerate(parts):
@@ -200,15 +274,93 @@
                     part = halo.at[own(low, size)]
                     pltpu.make_async_copy(part, part, halo_recv.at[k]).wait()
 
-        @pl.loop(0, chunks)
+        def send_run(ref, base, q, start, count, up, ahead):
+            for j in range(comp_count // 2):
+                home = jnp.where(up == ahead, comp_count // 2 + j, j)
+                source = ref.at[base + home, pl.ds(start, count)]
+                place = gathered.at[q, pl.ds(c * comp_local + start, count)]
+
+                @pl.when(home == c)
+                def _():
+                    pltpu.make_async_copy(source, place, there_recv.at[q]).start()
+
+                @pl.when(home != c)
+                def _():
+                    pltpu.make_async_remote_copy(
+                        src_ref=source,
+                        dst_ref=place,
+                        send_sem=there_send.at[q],
+                        recv_sem=there_recv.at[q],
+                        device_id=(home, l),
+                        device_id_type=MESH,
+                    ).start()
+
+        def by_halves(ref, q, wanted, ahead, before_send=None):
+            base = q * comp_count
+
+            def put(i, t, here, values, up):
+                ref[base + i * 2 + t, here, :] = values
+                ref[base + (rows - 1 - i) * 2 + t, here, :] = values
+
+            done = 0
+            for k in range(4):
+                need = comp_local if k == 3 else (k + 1) * quarter * RUN + rest
+                ready = min(-(-need // (8 * PAIR)), groups // PAIR)
+
+                @pl.loop(done, ready)
+                def _(g):
+                    for h in range(PAIR):
+                        advect_group(q, pl.multiple_of(g * (8 * PAIR) + h * 8, 8), wanted, put)
+
+                done = ready
+                if k == 3:
+                    for start in tail_groups:
+                        advect_group(q, start, wanted, put)
+                if before_send is not None and k == 0:
+                    before_send()
+
+                @pl.loop(k * quarter, (k + 1) * quarter)
+                def _(m):
+                    start, up = run_of(m)
+                    send_run(ref, base, q, start, RUN, up, ahead)
+
+                if before_send is not None and k == 0:
+                    after_first()
+
+            send_run(ref, base, q, rest_run[0], rest, rest_run[1], ahead)
+
+        for q in range(EARLY):
+            wait_cells(q)
+        for q in range(EARLY):
+            by_halves(early, q, (2, 3), True, meet if q == 0 else None)
+        for q in range(EARLY, chunks):
+            send_halos(q)
+        pltpu.make_async_copy(pair_in, map_in, map_sem.at[0]).start()
+        pltpu.make_async_copy(pair_out, map_out, map_sem.at[1]).start()
+        for q in range(EARLY):
+            wait_part(q)
+            by_halves(advected, q, (0, 1), False)
+
+        @pl.loop(EARLY, chunks)
         def _(q):
             wait_part(q)
-
-            @pl.loop(0, groups)
+            held = {}
+
+            def put(i, t, here, values, up):
+                held[i, t] = values
+                if i >= rows // 2:
+                    mirror = held[rows - 1 - i, t]
+                    base = q * comp_count + t
+                    advected[base + i * 2, here, :] = jnp.where(up, values, mirror)
+                    advected[base + (rows - 1 - i) * 2, here, :] = jnp.where(up, mirror, values)
+
+            @pl.loop(0, groups // PAIR)
             def _(g):
-                advect_group(q, pl.multiple_of(g * 8, 8))
-
-            advect_group(q, comp_local - 8)
+                for h in range(PAIR):
+                    advect_group(q, pl.multiple_of(g * (8 * PAIR) + h * 8, 8), (0, 1, 2, 3), put)
+
+            for start in tail_groups:
+                advect_group(q, start, (0, 1, 2, 3), put)
 
             place = gathered.at[q, pl.ds(c * comp_local, comp_local)]
             pltpu.make_async_copy(advected.at[q * comp_count + c], place, there_recv.at[q]).start()
@@ -224,6 +376,12 @@
                     device_id=(home, l),
                     device_id_type=MESH,
                 ).start()
+
+        for i, ref in enumerate((wind_input, whitecap)):
+            for low in range(0, total, LANE):
+                size = min(LANE, total - low)
+                rates_rows[i : i + 1, low : low + size] = ref[pl.ds(low, size)].reshape(1, size)
+        rates[...] = rates_rows[...].T
 
         pltpu.make_async_copy(pair_in, map_in, map_sem.at[0]).wait()
         pltpu.make_async_copy(pair_out, map_out, map_sem.at[1]).wait()
@@ -301,24 +459,6 @@
     comp_local, rows, lon = energy.shape
     total = comp_local * comp_count
     chunks = lon // CHUNK
-    lat_place = lax.axis_index("lat")
-    comp_place = lax.axis_index("comp")
-    comp_ids = comp_place * comp_local + jnp.arange(comp_local)
-    angles = 2.0 * math.pi * ((comp_ids % NDIR).astype(F32) + 0.5) / NDIR
-    speed_table = lax.dynamic_slice_in_dim(
-        jnp.repeat(group_speed, NDIR, axis=0), comp_place * comp_local, comp_local, 0
-    )
-    table = jnp.concatenate(
-        [speed_table, jnp.cos(angles)[:, None], jnp.sin(angles)[:, None]], axis=1
-    )
-    rates = jnp.stack([wind_input, whitecap], axis=1)
-
-    def band(x):
-        x = jnp.pad(x, ((SUB, SUB), (LANE, LANE)))
-        return lax.dynamic_slice_in_dim(x, lat_place * rows, rows + 2 * SUB, 0)
-
-    sea = band(sea_mask).astype(F32)
-    classes = band(depth_class)
     blocks = chunks * comp_count
     anywhere = pl.BlockSpec(memory_space=pl.ANY)
     near = pl.BlockSpec(memory_space=pltpu.VMEM)
@@ -326,11 +466,12 @@
     return pl.pallas_call(
         make_kernel(comp_count, lat_count, comp_local, rows, lon),
         out_shape=jax.ShapeDtypeStruct(energy.shape, F32),
-        in_specs=[anywhere] * 3 + [near] * 4,
+        in_specs=[anywhere] * 5 + [pl.BlockSpec(memory_space=pltpu.SMEM), near, near],
         out_specs=anywhere,
         scratch_shapes=[
             pltpu.VMEM((lon // LANE + 2, rows, comp_local, LANE), F32),
             pltpu.VMEM((lon // LANE + 2, 2, comp_local, LANE), F32),
+            pltpu.VMEM((EARLY * comp_count, comp_local, LANE), F32),
             pltpu.VMEM((blocks, comp_local, LANE), F32),
             pltpu.VMEM((chunks, total, LANE), F32),
             pltpu.VMEM((blocks, comp_local, LANE), F32),
@@ -338,7 +479,15 @@
             pltpu.VMEM((total, total), BF16),
             pltpu.VMEM((total, LANE), BF16),
             pltpu.VMEM((total, LANE), BF16),
-            dma((chunks,)),
+            pltpu.VMEM((16, lon), jnp.int32),
+            pltpu.VMEM((16, lon), jnp.int32),
+            pltpu.VMEM((rows + 2 * SUB, chunks * (CHUNK // LANE + 1), 8, LANE), F32),
+            pltpu.VMEM((rows + 2 * SUB, chunks * (CHUNK // LANE + 1), 8, LANE), jnp.int32),
+            pltpu.VMEM((8, total), F32),
+            pltpu.VMEM((total, 8), F32),
+            pltpu.VMEM((2, NDIR + 8, LANE), F32),
+            dma((chunks,)),
+            dma((2,)),
             dma((2,)),
             dma((chunks,)),
             dma((chunks,)),
@@ -354,7 +503,7 @@
         cost_estimate=pl.CostEstimate(
             flops=4 * total * total * chunks * LANE, bytes_accessed=24 * 2**20, transcendentals=0
         ),
-    )(energy, pair_in, pair_out, sea, classes, table, rates)
+    )(energy, pair_in, pair_out, sea_mask, depth_class, group_speed.T, wind_input, whitecap)
 
 
 def solution(mesh):

time: 162 us -> 140 us (0.86)
  Pallas kernels: 149 us -> 133 us
  local copies, waits for them, and re-layouts: 10.4 us -> 5.97 us
  other arithmetic: 1.7 us -> 0 us
    pallas_call x1, Pallas kernels: 149 us -> 133 us  [per_device(): pl.pallas_call(make_kernel(comp_count, lat_count, comp_local, rows, lon),...]
    another operation x3 -> x0, local copies, waits for them, and re-layouts: 2.67 us -> none  [per_device(): rates = jnp.stack([wind_input, whitecap], axis=1)]
where the time goes in v2:
time: 140 us; the launch traced here: 139 us
  Pallas kernels  133 us (95%)
  local copies, waits for them, and re-layouts  5.97 us (4%)
    pallas_call x1, Pallas kernels, per_device(): pl.pallas_call(make_kernel(comp_count, lat_count, comp_local, rows, lon),...  133 us
    unnamed x1, local copies, waits for them, and re-layouts  5.97 us

profile of v2, /device:TPU:1, one launch (start us, length us, event | category | flops | bytes accessed | tf_op | source)
XLA Modules:
  0.0 139.4 jit_solution(1869711985693186182)
XLA Ops:
  0.0 133.4 %shard_map.82 = f32[225,4,1536]{2,1,0:T(4,128)} custom-call(f32[225,4,1536]{2,1,0:T(4,128)} %energy.1, bf16[1800,1800]{1,0:T(8,128)(2,1)} %pair_in.1, bf16[1800,1800]{1,0:T(8,128)(2,1)} %pair_out.1, s32[64,1536]{1,0:T(8,128)} %sea_mask.1, s32[64,1536]{1,0:T(8,128)} %depth_class.1, f32[8,50]{1,0:T(8,128)} %bitcast.1, f32[1800]{0:T(1024)} %wind_input.1, ...), custom_call_target="tpu_custom_call" | custom-call | flops 9953280000 | bytes 25165824 | tf_op jit(solution)/shard_map/pallas_call | solution.py:466
  133.4 6.0 %copy.10 = f32[225,4,1536]{2,1,0:T(4,128)} copy(f32[225,4,1536]{2,1,0:T(4,128)} %shard_map.82) | data formatting | bytes 11059200

commit v3 on v2

--- a/solution.py
+++ b/solution.py
@@ -52,13 +52,12 @@
         group_speed,
         wind_input,
         whitecap,
-        out,
+        returned,
         cells,
         halo,
         early,
         advected,
         gathered,
-        returned,
         map_in,
         map_out,
         half,
@@ -79,7 +78,6 @@
         there_recv,
         back_send,
         back_recv,
-        out_sem,
     ):
         c = lax.axis_index("comp")
         l = lax.axis_index("lat")
@@ -112,7 +110,7 @@
         ]
         for copy in fact_copies:
             copy.start()
-        for q in range(chunks):
+        for q in range(EARLY - 1):
             load_cells(q)
 
         barrier = pltpu.get_barrier_semaphore()
@@ -156,6 +154,8 @@
                     for t in range(spread - 1):
                         ref[i, q * spread + t] = wide[first + 1 + t]
                     ref[i, q * spread + spread - 1] = edge(wide[first], wide[first + spread])
+        for q in range(EARLY - 1, chunks):
+            load_cells(q)
 
         def send_halo(start, count, up, q):
             low, size = parts[q]
@@ -183,7 +183,7 @@
         rest_run = ((1 - odd) * runs * RUN, lax.rem(c, 4) < 2)
 
         def send_halos(q):
-            if q >= EARLY:
+            if q > 0:
                 wait_cells(q)
 
             @pl.loop(0, runs)
@@ -192,13 +192,6 @@
                 send_halo(start, RUN, up, q)
 
             send_halo(rest_run[0], rest, rest_run[1], q)
-
-        def meet():
-            pl.semaphore_wait(barrier, comp_count + 1)
-
-        def after_first():
-            for q in range(EARLY):
-                send_halos(q)
 
         def advect_group(q, start, wanted, put):
             here = pl.ds(start, 8)
@@ -295,12 +288,18 @@
                         device_id_type=MESH,
                     ).start()
 
-        def by_halves(ref, q, wanted, ahead, before_send=None):
+        def by_halves(ref, q, wanted, ahead, opening=False):
             base = q * comp_count
 
             def put(i, t, here, values, up):
                 ref[base + i * 2 + t, here, :] = values
                 ref[base + (rows - 1 - i) * 2 + t, here, :] = values
+
+            def send_quarter(k):
+                @pl.loop(k * quarter, (k + 1) * quarter)
+                def _(m):
+                    start, up = run_of(m)
+                    send_run(ref, base, q, start, RUN, up, ahead)
 
             done = 0
             for k in range(4):
@@ -316,23 +315,20 @@
                 if k == 3:
                     for start in tail_groups:
                         advect_group(q, start, wanted, put)
-                if before_send is not None and k == 0:
-                    before_send()
-
-                @pl.loop(k * quarter, (k + 1) * quarter)
-                def _(m):
-                    start, up = run_of(m)
-                    send_run(ref, base, q, start, RUN, up, ahead)
-
-                if before_send is not None and k == 0:
-                    after_first()
+                if not opening or k > 1:
+                    send_quarter(k)
+                elif k == 1:
+                    pl.semaphore_wait(barrier, comp_count + 1)
+                    send_quarter(0)
+                    send_quarter(1)
+                    for part in range(EARLY):
+                        send_halos(part)
 
             send_run(ref, base, q, rest_run[0], rest, rest_run[1], ahead)
 
+        wait_cells(0)
         for q in range(EARLY):
-            wait_cells(q)
-        for q in range(EARLY):
-            by_halves(early, q, (2, 3), True, meet if q == 0 else None)
+            by_halves(early, q, (2, 3), True, opening=q == 0)
         for q in range(EARLY, chunks):
             send_halos(q)
         pltpu.make_async_copy(pair_in, map_in, map_sem.at[0]).start()
@@ -427,17 +423,8 @@
                     device_id_type=MESH,
                 ).start()
 
-        def write(q, i, t):
-            b = q * comp_count + i * 2 + t
-            return pltpu.make_async_copy(
-                returned.at[b], out.at[:, i, pl.ds(q * CHUNK + t * LANE, LANE)], out_sem.at[b]
-            )
-
         for q in range(chunks):
             pltpu.make_async_copy(gathered.at[q], gathered.at[q], back_recv.at[q]).wait()
-            for i in range(rows):
-                for t in range(CHUNK // LANE):
-                    write(q, i, t).start()
 
         sent = gathered.at[0, pl.ds(0, (comp_count - 1) * comp_local)]
         for q, (low, size) in enumerate(parts):
@@ -445,10 +432,24 @@
             pltpu.make_async_copy(sent, sent, back_send.at[q]).wait()
             part = halo.at[own(low, size)]
             pltpu.make_async_copy(part, part, halo_send.at[q]).wait()
-        for q in range(chunks):
-            for i in range(rows):
-                for t in range(CHUNK // LANE):
-                    write(q, i, t).wait()
+
+    return kernel
+
+
+def write_kernel(comp_count, rows, blocks):
+    def kernel(returned, out, sem):
+        copies = []
+        for b in range(blocks):
+            q, place = divmod(b, comp_count)
+            i, t = divmod(place, CHUNK // LANE)
+            lanes = pl.ds(q * CHUNK + t * LANE, LANE)
+            copies.append(
+                pltpu.make_async_copy(returned.at[b], out.at[:, i, lanes], sem.at[b])
+            )
+        for copy in copies:
+            copy.start()
+        for copy in copies:
+            copy.wait()
 
     return kernel
 
@@ -463,18 +464,17 @@
     anywhere = pl.BlockSpec(memory_space=pl.ANY)
     near = pl.BlockSpec(memory_space=pltpu.VMEM)
     dma = pltpu.SemaphoreType.DMA
-    return pl.pallas_call(
+    returned = pl.pallas_call(
         make_kernel(comp_count, lat_count, comp_local, rows, lon),
-        out_shape=jax.ShapeDtypeStruct(energy.shape, F32),
+        out_shape=pltpu.VMEM((blocks, comp_local, LANE), F32),
         in_specs=[anywhere] * 5 + [pl.BlockSpec(memory_space=pltpu.SMEM), near, near],
-        out_specs=anywhere,
+        out_specs=near,
         scratch_shapes=[
             pltpu.VMEM((lon // LANE + 2, rows, comp_local, LANE), F32),
             pltpu.VMEM((lon // LANE + 2, 2, comp_local, LANE), F32),
             pltpu.VMEM((EARLY * comp_count, comp_local, LANE), F32),
             pltpu.VMEM((blocks, comp_local, LANE), F32),
             pltpu.VMEM((chunks, total, LANE), F32),
-            pltpu.VMEM((blocks, comp_local, LANE), F32),
             pltpu.VMEM((total, total), BF16),
             pltpu.VMEM((total, total), BF16),
             pltpu.VMEM((total, LANE), BF16),
@@ -495,15 +495,22 @@
             dma((chunks,)),
             dma((chunks,)),
             dma((chunks,)),
-            dma((blocks,)),
         ],
         compiler_params=pltpu.CompilerParams(
-            collective_id=0, has_side_effects=True, vmem_limit_bytes=58 * 2**20
+            collective_id=0, has_side_effects=True, vmem_limit_bytes=50 * 2**20
         ),
         cost_estimate=pl.CostEstimate(
             flops=4 * total * total * chunks * LANE, bytes_accessed=24 * 2**20, transcendentals=0
         ),
     )(energy, pair_in, pair_out, sea_mask, depth_class, group_speed.T, wind_input, whitecap)
+    return pl.pallas_call(
+        write_kernel(comp_count, rows, blocks),
+        out_shape=jax.ShapeDtypeStruct(energy.shape, F32),
+        in_specs=[near],
+        out_specs=anywhere,
+        scratch_shapes=[dma((blocks,))],
+        compiler_params=pltpu.CompilerParams(vmem_limit_bytes=8 * 2**20),
+    )(returned)
 
 
 def solution(mesh):

time: 140 us -> 135 us (0.964)
  local copies, waits for them, and re-layouts: 5.97 us -> 0 us
    unnamed x1 -> x0, local copies, waits for them, and re-layouts: 5.97 us -> none
    pallas_call x0 -> x1, Pallas kernels: none -> 2.82 us  [per_device(): pl.pallas_call(write_kernel(comp_count, rows, blocks), out_shape=jax.Shap...]
    pallas_call x1, Pallas kernels: 133 us -> 132 us  [per_device(): pl.pallas_call(make_kernel(comp_count, lat_count, comp_local, rows, lon),...]
where the time goes in v3:
time: 135 us; the launch traced here: 134 us
  Pallas kernels  134 us (99%)
    pallas_call x1, Pallas kernels, per_device(): pl.pallas_call(make_kernel(comp_count, lat_count, comp_local, rows, lon),...  132 us
    pallas_call x1, Pallas kernels, per_device(): pl.pallas_call(write_kernel(comp_count, rows, blocks), out_shape=jax.Shap...  2.82 us

profile of v3, /device:TPU:1, one launch (start us, length us, event | category | flops | bytes accessed | tf_op | source)
XLA Modules:
  0.0 134.5 jit_solution(930720917116988207)
XLA Ops:
  0.0 131.6 %shard_map.82.returned = f32[48,225,128]{2,1,0:T(8,128)S(1)} custom-call(f32[225,4,1536]{2,1,0:T(4,128)} %energy.1, bf16[1800,1800]{1,0:T(8,128)(2,1)} %pair_in.1, bf16[1800,1800]{1,0:T(8,128)(2,1)} %pair_out.1, s32[64,1536]{1,0:T(8,128)} %sea_mask.1, s32[64,1536]{1,0:T(8,128)} %depth_class.1, f32[8,50]{1,0:T(8,128)} %bitcast.1, f32[1800]{0:T(1024)} %wind_input.1, ...), custom_call_target="tpu_custom_call" | custom-call | flops 9953280000 | bytes 25165824 | tf_op jit(solution)/shard_map/pallas_call | solution.py:467
  131.6 2.8 %shard_map.83 = f32[225,4,1536]{2,1,0:T(4,128)} custom-call(f32[48,225,128]{2,1,0:T(8,128)S(1)} %shard_map.82.returned), custom_call_target="tpu_custom_call" | custom-call | tf_op jit(solution)/shard_map/pallas_call | solution.py:506

commit v4 on v3

--- a/solution.py
+++ b/solution.py
@@ -19,7 +19,7 @@
 LANE = 128
 CHUNK = 256
 RUN = 18
-EARLY = 3
+EARLY = 4
 PAIR = 2
 
 
@@ -110,8 +110,7 @@
         ]
         for copy in fact_copies:
             copy.start()
-        for q in range(EARLY - 1):
-            load_cells(q)
+        load_cells(0)
 
         barrier = pltpu.get_barrier_semaphore()
         north = lax.rem(l + 1, lat_count)
@@ -154,7 +153,7 @@
                     for t in range(spread - 1):
                         ref[i, q * spread + t] = wide[first + 1 + t]
                     ref[i, q * spread + spread - 1] = edge(wide[first], wide[first + spread])
-        for q in range(EARLY - 1, chunks):
+        for q in range(1, chunks):
             load_cells(q)
 
         def send_halo(start, count, up, q):
@@ -288,7 +287,7 @@
                         device_id_type=MESH,
                     ).start()
 
-        def by_halves(ref, q, wanted, ahead, opening=False):
+        def by_halves(ref, q, wanted, ahead, first_halo=None):
             base = q * comp_count
 
             def put(i, t, here, values, up):
@@ -315,20 +314,17 @@
                 if k == 3:
                     for start in tail_groups:
                         advect_group(q, start, wanted, put)
-                if not opening or k > 1:
-                    send_quarter(k)
-                elif k == 1:
+                if first_halo == 0 and k == 0:
                     pl.semaphore_wait(barrier, comp_count + 1)
-                    send_quarter(0)
-                    send_quarter(1)
-                    for part in range(EARLY):
-                        send_halos(part)
+                send_quarter(k)
+                if first_halo is not None and k % 2 == 1:
+                    send_halos(first_halo + k // 2)
 
             send_run(ref, base, q, rest_run[0], rest, rest_run[1], ahead)
 
         wait_cells(0)
         for q in range(EARLY):
-            by_halves(early, q, (2, 3), True, opening=q == 0)
+            by_halves(early, q, (2, 3), True, 2 * q if q < EARLY // 2 else None)
         for q in range(EARLY, chunks):
             send_halos(q)
         pltpu.make_async_copy(pair_in, map_in, map_sem.at[0]).start()
@@ -406,7 +402,7 @@
                     wind * now - white * mean_energy * now + transfer
                 )
 
-            place = returned.at[q * comp_count + c]
+            place = returned.at[q * (CHUNK // LANE) + lax.rem(c, 2), :, c // 2]
             pltpu.make_async_copy(
                 gathered.at[q, pl.ds(c * comp_local, comp_local)], place, back_recv.at[q]
             ).start()
@@ -436,16 +432,14 @@
     return kernel
 
 
-def write_kernel(comp_count, rows, blocks):
+def write_kernel(tiles):
     def kernel(returned, out, sem):
-        copies = []
-        for b in range(blocks):
-            q, place = divmod(b, comp_count)
-            i, t = divmod(place, CHUNK // LANE)
-            lanes = pl.ds(q * CHUNK + t * LANE, LANE)
-            copies.append(
-                pltpu.make_async_copy(returned.at[b], out.at[:, i, lanes], sem.at[b])
+        copies = [
+            pltpu.make_async_copy(
+                returned.at[tile], out.at[:, :, pl.ds(tile * LANE, LANE)], sem.at[tile]
             )
+            for tile in range(tiles)
+        ]
         for copy in copies:
             copy.start()
         for copy in copies:
@@ -460,13 +454,13 @@
     comp_local, rows, lon = energy.shape
     total = comp_local * comp_count
     chunks = lon // CHUNK
-    blocks = chunks * comp_count
+    blocks, tiles = chunks * comp_count, lon // LANE
     anywhere = pl.BlockSpec(memory_space=pl.ANY)
     near = pl.BlockSpec(memory_space=pltpu.VMEM)
     dma = pltpu.SemaphoreType.DMA
     returned = pl.pallas_call(
         make_kernel(comp_count, lat_count, comp_local, rows, lon),
-        out_shape=pltpu.VMEM((blocks, comp_local, LANE), F32),
+        out_shape=pltpu.VMEM((tiles, comp_local, rows, LANE), F32),
         in_specs=[anywhere] * 5 + [pl.BlockSpec(memory_space=pltpu.SMEM), near, near],
         out_specs=near,
         scratch_shapes=[
@@ -504,11 +498,11 @@
         ),
     )(energy, pair_in, pair_out, sea_mask, depth_class, group_speed.T, wind_input, whitecap)
     return pl.pallas_call(
-        write_kernel(comp_count, rows, blocks),
+        write_kernel(tiles),
         out_shape=jax.ShapeDtypeStruct(energy.shape, F32),
         in_specs=[near],
         out_specs=anywhere,
-        scratch_shapes=[dma((blocks,))],
+        scratch_shapes=[dma((tiles,))],
         compiler_params=pltpu.CompilerParams(vmem_limit_bytes=8 * 2**20),
     )(returned)
 

time: 135 us -> 133 us (0.985)
  no operation moved by 1% of the time
where the time goes in v4:
time: 133 us
  Pallas kernels  133 us (100%)
    pallas_call x1, Pallas kernels, per_device(): pl.pallas_call(make_kernel(comp_count, lat_count, comp_local, rows, lon),...  131 us

profile of v4, /device:TPU:1, one launch (start us, length us, event | category | flops | bytes accessed | tf_op | source)
XLA Modules:
  0.0 133.3 jit_solution(13605008001080131246)
XLA Ops:
  0.0 130.6 %shard_map.82.returned = f32[12,225,4,128]{3,2,1,0:T(4,128)S(1)} custom-call(f32[225,4,1536]{2,1,0:T(4,128)} %energy.1, bf16[1800,1800]{1,0:T(8,128)(2,1)} %pair_in.1, bf16[1800,1800]{1,0:T(8,128)(2,1)} %pair_out.1, s32[64,1536]{1,0:T(8,128)} %sea_mask.1, s32[64,1536]{1,0:T(8,128)} %depth_class.1, f32[8,50]{1,0:T(8,128)} %bitcast.1, f32[1800]{0:T(1024)} %wind_input.1, ...), custom_call_target="tpu_custom_call" | custom-call | flops 9953280000 | bytes 25165824 | tf_op jit(solution)/shard_map/pallas_call | solution.py:461
  130.6 2.5 %shard_map.83 = f32[225,4,1536]{2,1,0:T(4,128)} custom-call(f32[12,225,4,128]{3,2,1,0:T(4,128)S(1)} %shard_map.82.returned), custom_call_target="tpu_custom_call" | custom-call | tf_op jit(solution)/shard_map/pallas_call | solution.py:500

commit v5 on v4

--- a/solution.py
+++ b/solution.py
@@ -39,8 +39,10 @@
     groups = comp_local // 8
     runs = comp_local // RUN
     rest = comp_local - runs * RUN
-    quarter = runs // 4
-    tail_groups = [*range(groups // PAIR * PAIR * 8, comp_local - 7, 8), comp_local - 8]
+    held_rows = pl.ds(0, comp_local)
+    tail_groups = range(groups // PAIR * PAIR * 8, comp_local, 8)
+    pieces = [runs * k // 4 for k in range(5)]
+    halo_after = {(0, 1): 0, (0, 3): 1, (1, 1): 2, (1, 3): 3}
     row_tiles = [(0, 448), (448, 448), (896, 448), (1344, total - 1344)]
 
     def kernel(
@@ -92,13 +94,13 @@
                 for r in range(rows):
                     pltpu.make_async_copy(
                         energy.at[:, r, pl.ds(tile * LANE, LANE)],
-                        cells.at[tile + 1, r],
+                        cells.at[tile + 1, r, held_rows],
                         load_sem.at[q],
                     ).start()
 
         def wait_cells(q):
             low, size = parts[q]
-            part = cells.at[own(low, size)]
+            part = cells.at[own(low, size), :, held_rows]
             pltpu.make_async_copy(part, part, load_sem.at[q]).wait()
 
         lat_rows = lat_count * rows
@@ -199,7 +201,7 @@
             first_tile = q * spread
             sublane = lax.broadcasted_iota(jnp.int32, (8, LANE), 0)
             low_freq = ident // NDIR
-            high_freq = (ident + 7) // NDIR
+            high_freq = jnp.minimum((ident + 7) // NDIR, group_speed.shape[1] - 1)
             later = sublane + lax.rem(ident, NDIR) >= NDIR
 
             def wide(v):
@@ -263,7 +265,7 @@
 
                 @pl.when(q == k)
                 def _():
-                    part = halo.at[own(low, size)]
+                    part = halo.at[own(low, size), :, held_rows]
                     pltpu.make_async_copy(part, part, halo_recv.at[k]).wait()
 
         def send_run(ref, base, q, start, count, up, ahead):
@@ -287,22 +289,22 @@
                         device_id_type=MESH,
                     ).start()
 
-        def by_halves(ref, q, wanted, ahead, first_halo=None):
+        def by_halves(ref, q, wanted, ahead):
             base = q * comp_count
 
             def put(i, t, here, values, up):
                 ref[base + i * 2 + t, here, :] = values
                 ref[base + (rows - 1 - i) * 2 + t, here, :] = values
 
-            def send_quarter(k):
-                @pl.loop(k * quarter, (k + 1) * quarter)
+            def send_piece(k):
+                @pl.loop(pieces[k], pieces[k + 1])
                 def _(m):
                     start, up = run_of(m)
                     send_run(ref, base, q, start, RUN, up, ahead)
 
             done = 0
             for k in range(4):
-                need = comp_local if k == 3 else (k + 1) * quarter * RUN + rest
+                need = comp_local if k == 3 else pieces[k + 1] * RUN + rest
                 ready = min(-(-need // (8 * PAIR)), groups // PAIR)
 
                 @pl.loop(done, ready)
@@ -314,17 +316,17 @@
                 if k == 3:
                     for start in tail_groups:
                         advect_group(q, start, wanted, put)
-                if first_halo == 0 and k == 0:
+                if ahead and q == 0 and k == 0:
                     pl.semaphore_wait(barrier, comp_count + 1)
-                send_quarter(k)
-                if first_halo is not None and k % 2 == 1:
-                    send_halos(first_halo + k // 2)
+                send_piece(k)
+                if ahead and (q, k) in halo_after:
+                    send_halos(halo_after[q, k])
 
             send_run(ref, base, q, rest_run[0], rest, rest_run[1], ahead)
 
         wait_cells(0)
         for q in range(EARLY):
-            by_halves(early, q, (2, 3), True, 2 * q if q < EARLY // 2 else None)
+            by_halves(early, q, (2, 3), True)
         for q in range(EARLY, chunks):
             send_halos(q)
         pltpu.make_async_copy(pair_in, map_in, map_sem.at[0]).start()
@@ -355,13 +357,15 @@
                 advect_group(q, start, (0, 1, 2, 3), put)
 
             place = gathered.at[q, pl.ds(c * comp_local, comp_local)]
-            pltpu.make_async_copy(advected.at[q * comp_count + c], place, there_recv.at[q]).start()
+            pltpu.make_async_copy(
+                advected.at[q * comp_count + c, held_rows], place, there_recv.at[q]
+            ).start()
 
             @pl.loop(1, comp_count)
             def _(d):
                 home = lax.rem(c + d, comp_count)
                 pltpu.make_async_remote_copy(
-                    src_ref=advected.at[q * comp_count + home],
+                    src_ref=advected.at[q * comp_count + home, held_rows],
                     dst_ref=place,
                     send_sem=there_send.at[q],
                     recv_sem=there_recv.at[q],
@@ -426,7 +430,7 @@
         for q, (low, size) in enumerate(parts):
             pltpu.make_async_copy(sent, sent, there_send.at[q]).wait()
             pltpu.make_async_copy(sent, sent, back_send.at[q]).wait()
-            part = halo.at[own(low, size)]
+            part = halo.at[own(low, size), :, held_rows]
             pltpu.make_async_copy(part, part, halo_send.at[q]).wait()
 
     return kernel
@@ -455,6 +459,7 @@
     total = comp_local * comp_count
     chunks = lon // CHUNK
     blocks, tiles = chunks * comp_count, lon // LANE
+    padded = -(-comp_local // 8) * 8
     anywhere = pl.BlockSpec(memory_space=pl.ANY)
     near = pl.BlockSpec(memory_space=pltpu.VMEM)
     dma = pltpu.SemaphoreType.DMA
@@ -464,10 +469,10 @@
         in_specs=[anywhere] * 5 + [pl.BlockSpec(memory_space=pltpu.SMEM), near, near],
         out_specs=near,
         scratch_shapes=[
-            pltpu.VMEM((lon // LANE + 2, rows, comp_local, LANE), F32),
-            pltpu.VMEM((lon // LANE + 2, 2, comp_local, LANE), F32),
-            pltpu.VMEM((EARLY * comp_count, comp_local, LANE), F32),
-            pltpu.VMEM((blocks, comp_local, LANE), F32),
+            pltpu.VMEM((lon // LANE + 2, rows, padded, LANE), F32),
+            pltpu.VMEM((lon // LANE + 2, 2, padded, LANE), F32),
+            pltpu.VMEM((EARLY * comp_count, padded, LANE), F32),
+            pltpu.VMEM((blocks, padded, LANE), F32),
             pltpu.VMEM((chunks, total, LANE), F32),
             pltpu.VMEM((total, total), BF16),
             pltpu.VMEM((total, total), BF16),

time: 133 us -> 134 us (level)
  no operation moved by 1% of the time
where the time goes in v5:
time: 134 us; the launch traced here: 133 us
  Pallas kernels  133 us (99%)
    pallas_call x1, Pallas kernels, per_device(): pl.pallas_call(make_kernel(comp_count, lat_count, comp_local, rows, lon),...  131 us

profile of v5, /device:TPU:1, one launch (start us, length us, event | category | flops | bytes accessed | tf_op | source)
XLA Modules:
  0.0 133.3 jit_solution(10037947445212149431)
XLA Ops:
  0.0 130.6 %shard_map.82.returned = f32[12,225,4,128]{3,2,1,0:T(4,128)S(1)} custom-call(f32[225,4,1536]{2,1,0:T(4,128)} %energy.1, bf16[1800,1800]{1,0:T(8,128)(2,1)} %pair_in.1, bf16[1800,1800]{1,0:T(8,128)(2,1)} %pair_out.1, s32[64,1536]{1,0:T(8,128)} %sea_mask.1, s32[64,1536]{1,0:T(8,128)} %depth_class.1, f32[8,50]{1,0:T(8,128)} %bitcast.1, f32[1800]{0:T(1024)} %wind_input.1, ...), custom_call_target="tpu_custom_call" | custom-call | flops 9953280000 | bytes 25165824 | tf_op jit(solution)/shard_map/pallas_call | solution.py:466
  130.6 2.5 %shard_map.83 = f32[225,4,1536]{2,1,0:T(4,128)} custom-call(f32[12,225,4,128]{3,2,1,0:T(4,128)S(1)} %shard_map.82.returned), custom_call_target="tpu_custom_call" | custom-call | tf_op jit(solution)/shard_map/pallas_call | solution.py:505

commit v6 on v5

--- a/solution.py
+++ b/solution.py
@@ -88,20 +88,33 @@
         def own(low, size):
             return pl.ds(low + 1, size)
 
-        def load_cells(q):
+        def load_cells(q, some=held_rows, sem=None):
             low, size = parts[q]
             for tile in range(low, low + size):
                 for r in range(rows):
                     pltpu.make_async_copy(
-                        energy.at[:, r, pl.ds(tile * LANE, LANE)],
-                        cells.at[tile + 1, r, held_rows],
-                        load_sem.at[q],
+                        energy.at[some, r, pl.ds(tile * LANE, LANE)],
+                        cells.at[tile + 1, r, some],
+                        load_sem.at[q if sem is None else sem],
                     ).start()
 
-        def wait_cells(q):
+        def wait_cells(q, some=held_rows, sem=None):
             low, size = parts[q]
-            part = cells.at[own(low, size), :, held_rows]
-            pltpu.make_async_copy(part, part, load_sem.at[q]).wait()
+            part = cells.at[own(low, size), :, some]
+            pltpu.make_async_copy(part, part, load_sem.at[q if sem is None else sem]).wait()
+
+        opening = -(-(pieces[1] * RUN + rest) // (8 * PAIR)) * (8 * PAIR)
+        opening_rows, other_rows = pl.ds(0, opening), pl.ds(opening, comp_local - opening)
+
+        barrier = pltpu.get_barrier_semaphore()
+        north = lax.rem(l + 1, lat_count)
+        south = lax.rem(l + lat_count - 1, lat_count)
+        for d in range(1, comp_count):
+            pl.semaphore_signal(
+                barrier, inc=1, device_id=(lax.rem(c + d, comp_count), l), device_id_type=MESH
+            )
+        for other in (north, south):
+            pl.semaphore_signal(barrier, inc=1, device_id=(c, other), device_id_type=MESH)
 
         lat_rows = lat_count * rows
         fact_low = jnp.clip((l * rows - SUB + 8) // 8 - 1, 0, lat_rows // 8 - 2) * 8
@@ -112,17 +125,7 @@
         ]
         for copy in fact_copies:
             copy.start()
-        load_cells(0)
-
-        barrier = pltpu.get_barrier_semaphore()
-        north = lax.rem(l + 1, lat_count)
-        south = lax.rem(l + lat_count - 1, lat_count)
-        for d in range(1, comp_count):
-            pl.semaphore_signal(
-                barrier, inc=1, device_id=(lax.rem(c + d, comp_count), l), device_id_type=MESH
-            )
-        for other in (north, south):
-            pl.semaphore_signal(barrier, inc=1, device_id=(c, other), device_id_type=MESH)
+        load_cells(0, opening_rows)
 
         angles = 2.0 * math.pi * (np.arange(trig.shape[1]) % NDIR + 0.5) / NDIR
         for i, values in enumerate((np.cos(angles), np.sin(angles))):
@@ -155,6 +158,7 @@
                     for t in range(spread - 1):
                         ref[i, q * spread + t] = wide[first + 1 + t]
                     ref[i, q * spread + spread - 1] = edge(wide[first], wide[first + spread])
+        load_cells(0, other_rows, chunks)
         for q in range(1, chunks):
             load_cells(q)
 
@@ -319,12 +323,14 @@
                 if ahead and q == 0 and k == 0:
                     pl.semaphore_wait(barrier, comp_count + 1)
                 send_piece(k)
+                if ahead and q == 0 and k == 0:
+                    wait_cells(0, other_rows, chunks)
                 if ahead and (q, k) in halo_after:
                     send_halos(halo_after[q, k])
 
             send_run(ref, base, q, rest_run[0], rest, rest_run[1], ahead)
 
-        wait_cells(0)
+        wait_cells(0, opening_rows)
         for q in range(EARLY):
             by_halves(early, q, (2, 3), True)
         for q in range(EARLY, chunks):
@@ -485,7 +491,7 @@
             pltpu.VMEM((8, total), F32),
             pltpu.VMEM((total, 8), F32),
             pltpu.VMEM((2, NDIR + 8, LANE), F32),
-            dma((chunks,)),
+            dma((chunks + 1,)),
             dma((2,)),
             dma((2,)),
             dma((chunks,)),

time: 134 us -> 133 us (level)
  no operation moved by 1% of the time
where the time goes in v6:
time: 133 us
  Pallas kernels  133 us (100%)
    pallas_call x1, Pallas kernels, per_device(): pl.pallas_call(make_kernel(comp_count, lat_count, comp_local, rows, lon),...  131 us

profile of v6, /device:TPU:1, one launch (start us, length us, event | category | flops | bytes accessed | tf_op | source)
XLA Modules:
  0.0 133.3 jit_solution(11624037354192957539)
XLA Ops:
  0.0 130.6 %shard_map.82.returned = f32[12,225,4,128]{3,2,1,0:T(4,128)S(1)} custom-call(f32[225,4,1536]{2,1,0:T(4,128)} %energy.1, bf16[1800,1800]{1,0:T(8,128)(2,1)} %pair_in.1, bf16[1800,1800]{1,0:T(8,128)(2,1)} %pair_out.1, s32[64,1536]{1,0:T(8,128)} %sea_mask.1, s32[64,1536]{1,0:T(8,128)} %depth_class.1, f32[8,50]{1,0:T(8,128)} %bitcast.1, f32[1800]{0:T(1024)} %wind_input.1, ...), custom_call_target="tpu_custom_call" | custom-call | flops 9953280000 | bytes 25165824 | tf_op jit(solution)/shard_map/pallas_call | solution.py:472
  130.6 2.5 %shard_map.83 = f32[225,4,1536]{2,1,0:T(4,128)} custom-call(f32[12,225,4,128]{3,2,1,0:T(4,128)S(1)} %shard_map.82.returned), custom_call_target="tpu_custom_call" | custom-call | tf_op jit(solution)/shard_map/pallas_call | solution.py:511

commit v7 on v5

--- a/solution.py
+++ b/solution.py
@@ -20,7 +20,7 @@
 CHUNK = 256
 RUN = 18
 EARLY = 4
-PAIR = 2
+PAIR = 4
 
 
 def sections(lon):

time: 134 us -> 133 us (level)
  no operation moved by 1% of the time
where the time goes in v7:
time: 133 us
  Pallas kernels  133 us (100%)
    pallas_call x1, Pallas kernels, per_device(): pl.pallas_call(make_kernel(comp_count, lat_count, comp_local, rows, lon),...  130 us

profile of v7, /device:TPU:1, one launch (start us, length us, event | category | flops | bytes accessed | tf_op | source)
XLA Modules:
  0.0 133.1 jit_solution(1579588730254551347)
XLA Ops:
  0.0 130.4 %shard_map.82.returned = f32[12,225,4,128]{3,2,1,0:T(4,128)S(1)} custom-call(f32[225,4,1536]{2,1,0:T(4,128)} %energy.1, bf16[1800,1800]{1,0:T(8,128)(2,1)} %pair_in.1, bf16[1800,1800]{1,0:T(8,128)(2,1)} %pair_out.1, s32[64,1536]{1,0:T(8,128)} %sea_mask.1, s32[64,1536]{1,0:T(8,128)} %depth_class.1, f32[8,50]{1,0:T(8,128)} %bitcast.1, f32[1800]{0:T(1024)} %wind_input.1, ...), custom_call_target="tpu_custom_call" | custom-call | flops 9953280000 | bytes 25165824 | tf_op jit(solution)/shard_map/pallas_call | solution.py:466
  130.4 2.5 %shard_map.83 = f32[225,4,1536]{2,1,0:T(4,128)} custom-call(f32[12,225,4,128]{3,2,1,0:T(4,128)S(1)} %shard_map.82.returned), custom_call_target="tpu_custom_call" | custom-call | tf_op jit(solution)/shard_map/pallas_call | solution.py:505
